TPU v7x, 32 devices: a whole 2x2x4 slice. The times are simulated.
32 devices in a mesh: groups: 2 (over x), expert: 8 (over z, y), dp: 2 (over core).
Axes of the slice: x: 2, y: 2, z: 4, core: 2. Of those that a mesh axis runs over, the one named last changes fastest.
Arguments:
- tokens: bfloat16 [4096, 2048], P(('groups', 'expert', 'dp')), parts along dimension 0, may hold values from -6 to 6
- routes: int32 [4096, 8], P(('groups', 'expert', 'dp')), parts along dimension 0, may hold values from 0 to 15, all different within a row; in each aligned block of 128 rows (0 to 127, 128 to 255, ...) at most 96 rows name the same one
- gate_levels: int32 [4096, 8], P(('groups', 'expert', 'dp')), parts along dimension 0, may hold values from 1 to 15
- w_gate: bfloat16 [16, 2048, 768], P(('expert', 'dp')), may hold values from -0.125 to 0.125
- w_up: bfloat16 [16, 2048, 768], P(('expert', 'dp')), may hold values from -0.125 to 0.125
- w_down: bfloat16 [16, 768, 2048], P(('expert', 'dp')), may hold values from -0.21875 to 0.21875
Outputs:
- mixed: bfloat16 [4096, 2048], P(('groups', 'expert', 'dp')), parts along dimension 0
There are 2 independent parts, one for each index of `groups`. A program takes and returns all parts, laid end to end along the dimension named above; an argument that names none is the same for every part. Nothing has to cross between parts.
Inputs may be any that keep to these rules, and one draw needn't show every extreme that they name: `routes`: among the 128 rows of one device, each expert is named by at most 96 rows; in every draw some device's rows name some expert exactly 96 times.
All inputs are finite; a program needn't handle non-finite values.
Results may differ from a plain program's by a relative error of at most 0.0057.
Values may be sent and summed in bfloat16 or wider, within the bound.
A program may use at most 64 MiB of HBM per device.

v0:
```python
import jax
import jax.numpy as jnp
from jax import lax
from jax.sharding import PartitionSpec as P


def per_device(tokens, routes, gate_levels, w_gate, w_up, w_down):
    tok_rows, model_dim = tokens.shape
    top_count = routes.shape[1]
    n_expert = lax.axis_size("expert")
    n_dp = lax.axis_size("dp")
    experts = n_expert * n_dp
    capacity = 3 * tok_rows * top_count // (2 * experts)
    route_list = routes.reshape(-1)
    marked = (route_list[:, None] == jnp.arange(experts, dtype=jnp.int32)[None, :]).astype(
        jnp.int32
    )
    earlier = jnp.cumsum(marked, axis=0) - marked
    position = jnp.sum(earlier * marked, axis=1)
    target = route_list * capacity + position
    owner_row = jnp.arange(route_list.shape[0], dtype=jnp.int32) // top_count
    source_row = jnp.zeros((experts * capacity,), jnp.int32).at[target].set(owner_row)
    filled = jnp.zeros((experts * capacity,), tokens.dtype).at[target].set(1)
    outgoing = (tokens[source_row] * filled[:, None]).reshape(experts, capacity, model_dim)
    arrived = lax.all_to_all(outgoing, ("expert", "dp"), split_axis=0, concat_axis=0, tiled=True)
    inputs = arrived.reshape(-1, model_dim)
    gate_act = jnp.dot(inputs, w_gate[0], preferred_element_type=jnp.float32)
    up_act = jnp.dot(inputs, w_up[0], preferred_element_type=jnp.float32)
    hidden = (jax.nn.silu(gate_act) * up_act).astype(jnp.bfloat16)
    produced = jnp.dot(hidden, w_down[0], preferred_element_type=jnp.float32).astype(jnp.bfloat16)
    returned = lax.all_to_all(
        produced.reshape(arrived.shape), ("expert", "dp"), split_axis=0, concat_axis=0, tiled=True
    )
    rows_back = returned.reshape(-1, model_dim)[target].reshape(tok_rows, top_count, model_dim)
    levels = gate_levels.astype(jnp.float32)
    weights = levels / jnp.sum(levels, axis=1, keepdims=True)
    mixed = jnp.sum(rows_back.astype(jnp.float32) * weights[:, :, None], axis=1)
    return mixed.astype(jnp.bfloat16)


def solution(mesh):
    in_specs = (
        P(("groups", "expert", "dp"), None),
        P(("groups", "expert", "dp"), None),
        P(("groups", "expert", "dp"), None),
        P(("expert", "dp"), None, None),
        P(("expert", "dp"), None, None),
        P(("expert", "dp"), None, None),
    )
    out_specs = P(("groups", "expert", "dp"), None)
    return jax.shard_map(
        per_device, mesh=mesh, in_specs=in_specs, out_specs=out_specs, check_vma=False
    )
```

profile of v0, /device:TPU:15, one launch (start us, length us, event | category | flops | bytes accessed | tf_op | source)
XLA Modules:
  0.0 360.6 jit_solution(1891062422638289334)
XLA Ops:
  0.0 0.9 copy.11
  0.9 0.1 eq.29
  1.0 0.1 eq.25
  1.1 0.7 broadcast_multiply_fusion.1
  1.8 4.5 %reduce-window.6 = s32[16,8,128]{2,1,0:T(8,128)S(1)} reduce-window(s32[16,8,128]{2,1,0:T(8,128)S(1)} %fusion.8, s32[]{:T(128)} %constant.28.clone.1), window={size=1x1x128 pad=0_0x0_0x127_0}, to_apply=%region_0.0 | reduce-window | flops 2080768 | bytes 131076 | tf_op jit(solution)/shard_map/reduce-window
  6.3 0.1 slice.12
  6.4 0.1 copy.13
  6.7 0.1 broadcast_add_fusion
  6.8 0.1 copy.10
  6.9 0.1 mul.47
  7.0 4.3 %scatter_custom_fusion = s32[1536]{0:T(1024)S(1)} fusion(s32[1024]{0:T(1024)S(1)} %bitcast.46, s32[1024]{0:T(1024)S(1)} %add_select_fusion, s32[]{:T(128)} %constant.28.clone.1), kind=kCustom, calls=%fused_computation.32 | custom fusion | bytes 6148 | tf_op jit(solution)/shard_map/scatter | solution.py:22
  11.4 7.6 %scatter_custom_fusion.1 = bf16[1536]{0:T(1024)(128)(2,1)S(1)} fusion(s32[1024]{0:T(1024)S(1)} %bitcast.47, bf16[1024]{0:T(1024)(128)(2,1)S(1)} %broadcast.67, bf16[]{:T(256)} %constant.36.clone.1), kind=kCustom, calls=%fused_computation.36 | custom fusion | bytes 3074 | tf_op jit(solution)/shard_map/scatter | solution.py:23
  19.0 0.1 mul.49
  19.1 13.8 %gather_fusion = bf16[1536,2048]{1,0:T(8,128)(2,1)} fusion(bf16[128,2048]{1,0:T(8,128)(2,1)} %param.6, s32[2048]{0:T(1024)S(1)} %pad_clamp_fusion), kind=kCustom, calls=%fused_computation | custom fusion | bytes 12589056 | tf_op jit(solution)/shard_map/gather | solution.py:24
  32.9 3.3 broadcast_multiply_fusion
  36.2 143.8 %all_to_all.10 = bf16[16,96,2048]{2,1,0:T(8,128)(2,1)S(1)} all-to-all(bf16[16,96,2048]{2,1,0:T(8,128)(2,1)S(1)} %broadcast_multiply_fusion), channel_id=1, replica_groups=mesh['groups'=2,'expert'=8,'dp'=2] {'expert','dp'}, dimensions={0} | all-to-all | bytes 12582912 | tf_op jit(solution)/shard_map/all_to_all | solution.py:25
  180.0 5.2 %fusion.3 = f32[1536,768]{1,0:T(8,128)S(1)} fusion(bf16[1536,2048]{1,0:T(8,128)(2,1)S(1)} %bitcast.41, bf16[1,2048,768]{2,1,0:T(8,128)(2,1)S(1)} %copy-done.2), kind=kOutput, calls=%fused_computation.10 | convolution fusion | flops 4831838208 | bytes 14155776 | tf_op jit(solution)/shard_map/dot_general | solution.py:27
  185.2 5.6 %multiply_convert_fusion = bf16[1536,768]{1,0:T(8,128)(2,1)S(1)} fusion(f32[1536,768]{1,0:T(8,128)S(1)} %fusion.3, bf16[1536,2048]{1,0:T(8,128)(2,1)S(1)} %bitcast.42, bf16[1,2048,768]{2,1,0:T(8,128)(2,1)S(1)} %copy-done.3), kind=kOutput, calls=%fused_computation.7 | convolution fusion | flops 4838916096 | bytes 16515072 | tf_op jit(solution)/shard_map/dot_general | solution.py:28
  190.8 7.0 %convolution_convert_fusion = bf16[1536,2048]{1,0:T(8,128)(2,1)} fusion(bf16[1536,768]{1,0:T(8,128)(2,1)S(1)} %multiply_convert_fusion, bf16[1,768,2048]{2,1,0:T(8,128)(2,1)S(1)} %copy-done), kind=kOutput, calls=%fused_computation.6 | convolution fusion | flops 4834983936 | bytes 11796480 | tf_op jit(solution)/shard_map/dot_general | solution.py:30
  197.9 5.6 %all-to-all-start.1 = ((bf16[16,96,2048]{2,1,0:T(8,128)(2,1)}), bf16[16,96,2048]{2,1,0:T(8,128)(2,1)}, u32[]{:S(2)}, u32[]{:S(2)}) async-start(bf16[16,96,2048]{2,1,0:T(8,128)(2,1)} %bitcast.40), calls=%async_computation.1 | async-start | bytes 12582912 | tf_op jit(solution)/shard_map/all_to_all | solution.py:31
  203.5 0.1 copy.15
  203.6 137.3 %all-to-all-done.1 = bf16[16,96,2048]{2,1,0:T(8,128)(2,1)} async-done(((bf16[16,96,2048]{2,1,0:T(8,128)(2,1)}), bf16[16,96,2048]{2,1,0:T(8,128)(2,1)}, u32[]{:S(2)}, u32[]{:S(2)}) %all-to-all-start.1) | async-done | bytes 6291488 | tf_op jit(solution)/shard_map/all_to_all | solution.py:31
  340.9 12.4 %gather_fusion.1 = bf16[1024,2048]{1,0:T(8,128)(2,1)} fusion(bf16[1536,2048]{1,0:T(8,128)(2,1)} %bitcast.10, s32[1024]{0:T(1024)S(1)} %broadcast_clamp_fusion), kind=kCustom, calls=%fused_computation.1 | custom fusion | bytes 8392704 | tf_op jit(solution)/shard_map/gather | solution.py:34
  353.3 7.3 %fusion = bf16[128,2048]{1,0:T(8,128)(2,1)} fusion(bf16[1024,2048]{1,0:T(8,128)(2,1)} %gather_fusion.1, f32[128,8]{1,0:T(8,128)S(1)} %copy.15), kind=kLoop, calls=%fused_computation.5 | loop fusion | flops 6029312 | bytes 4722688 | tf_op jit(solution)/shard_map/reduce_sum | solution.py:37
  (21 shorter events, 0.2 us)
Async XLA Ops:
  0.0 190.8 %copy-start = (bf16[1,768,2048]{2,1,0:T(8,128)(2,1)S(1)}, bf16[1,768,2048]{2,1,0:T(8,128)(2,1)}, u32[]{:S(2)}) copy-start(bf16[1,768,2048]{2,1,0:T(8,128)(2,1)} %param.11) | copy-start | bytes 9437188
  36.2 143.8 %copy-start.2 = (bf16[1,2048,768]{2,1,0:T(8,128)(2,1)S(1)}, bf16[1,2048,768]{2,1,0:T(8,128)(2,1)}, u32[]{:S(2)}) copy-start(bf16[1,2048,768]{2,1,0:T(8,128)(2,1)} %param.9) | copy-start | bytes 9437188
  180.0 5.2 %copy-start.3 = (bf16[1,2048,768]{2,1,0:T(8,128)(2,1)S(1)}, bf16[1,2048,768]{2,1,0:T(8,128)(2,1)}, u32[]{:S(2)}) copy-start(bf16[1,2048,768]{2,1,0:T(8,128)(2,1)} %param.10) | copy-start | bytes 9437188
  197.9 5.6 %copy-start.1 = (s32[128,8]{0,1:T(8,128)S(1)}, s32[128,8]{0,1:T(8,128)}, u32[]{:S(2)}) copy-start(s32[128,8]{0,1:T(8,128)} %param.8) | copy-start | bytes 12292
  197.9 143.0 %all-to-all-start.1 = ((bf16[16,96,2048]{2,1,0:T(8,128)(2,1)}), bf16[16,96,2048]{2,1,0:T(8,128)(2,1)}, u32[]{:S(2)}, u32[]{:S(2)}) async-start(bf16[16,96,2048]{2,1,0:T(8,128)(2,1)} %bitcast.40), calls=%async_computation.1 | async-start | bytes 12582912 | tf_op jit(solution)/shard_map/all_to_all | solution.py:31
where the time goes:
time: 361 us
  blocking collectives  144 us (40%)
  waiting for transfers between devices  137 us (38%)
  local copies, waits for them, and re-layouts  40 us (11%)
  matrix products  17.8 us (5%)
  other arithmetic  16 us (4%)
  starting transfers between devices  5.64 us (2%)
    all_to_all x1, blocking collectives, per_device(): lax.all_to_all(outgoing, ('expert', 'dp'), split_axis=0, concat_axis=0, t...  144 us
    all_to_all x1, waiting for transfers between devices, per_device(): lax.all_to_all(produced.reshape(arrived.shape), ('expert', 'dp'), split_a...  137 us
    gather x1, local copies, waits for them, and re-layouts, per_device(): tokens[source_row] * filled[:, None]  13.8 us
    gather x1, local copies, waits for them, and re-layouts, per_device(): returned.reshape(-1, model_dim)[target]  12.4 us
    scatter x1, local copies, waits for them, and re-layouts, per_device(): filled = jnp.zeros((experts * capacity,), tokens.dtype).at[target].set(1)  7.59 us
    reduce_sum x1, other arithmetic, per_device(): mixed = jnp.sum(rows_back.astype(jnp.float32) * weights[:, :, None], axis=1)  7.32 us
  transfers between devices with their start and end apart: 1, of which 1 were waited for; matrix products, arithmetic and copies ran while one was open for 0% of the time, Pallas kernels for 0%

commit v1 on v0

v1 whole, which is shorter than its diff:
```python
import jax
import jax.numpy as jnp
from jax import lax
from jax.sharding import PartitionSpec as P

AXES = ("expert", "dp")


def expert_part(x, factor, w_gate, w_up, w_down):
    gate_act = jnp.dot(x, w_gate, preferred_element_type=jnp.float32)
    up_act = jnp.dot(x, w_up, preferred_element_type=jnp.float32)
    hidden = (jax.nn.silu(gate_act) * up_act).astype(jnp.bfloat16)
    produced = jnp.dot(hidden, w_down, preferred_element_type=jnp.float32)
    return (produced * factor).astype(jnp.bfloat16)


def per_device(tokens, routes, gate_levels, w_gate, w_up, w_down):
    rows, width = tokens.shape
    devices = lax.axis_size("expert") * lax.axis_size("dp")
    me = lax.axis_index("expert") * lax.axis_size("dp") + lax.axis_index("dp")
    named = routes[:, :, None] == jnp.arange(devices, dtype=jnp.int32)[None, None, :]
    levels = gate_levels.astype(jnp.float32)
    weights = levels / jnp.sum(levels, axis=1, keepdims=True)
    spread = jnp.sum(jnp.where(named, weights[:, :, None], 0.0), axis=1)
    factors = lax.all_gather(spread, AXES, axis=0, tiled=False)
    mine = lax.dynamic_index_in_dim(factors, me, 2, keepdims=True)
    chunks = 2 if devices <= 16 else 8
    step = rows // chunks
    results = []
    for c in range(chunks):
        part = slice(c * step, (c + 1) * step)
        block = tokens[part]
        if devices > 16 and c > 0:
            block, _ = lax.optimization_barrier((block, results[-1]))
        x = lax.all_gather(block, AXES, axis=0, tiled=True)
        y = expert_part(x, mine[:, part].reshape(-1, 1), w_gate[0], w_up[0], w_down[0])
        results.append(lax.psum_scatter(y, AXES, scatter_dimension=0, tiled=True))
    return jnp.concatenate(results, axis=0)


def solution(mesh):
    token_spec = P(("groups", "expert", "dp"), None)
    weight_spec = P(("expert", "dp"), None, None)
    return jax.shard_map(
        per_device,
        mesh=mesh,
        in_specs=(token_spec,) * 3 + (weight_spec,) * 3,
        out_specs=token_spec,
        check_vma=False,
    )
```

time: 361 us -> 274 us (0.76)
  the two profiles are of different devices: /device:TPU:15 before, /device:TPU:0 now
where the time goes in v1:
time: 274 us
  waiting for transfers between devices  189 us (69%)
  matrix products  41.5 us (15%)
  blocking collectives  23.5 us (9%)
  between operations  13.1 us (5%)
  other arithmetic  3.97 us (1%)
    reduce_scatter x2, waiting for transfers between devices, per_device(): results.append(lax.psum_scatter(y, AXES, scatter_dimension=0, tiled=True))  130 us
    all_gather x2, waiting for transfers between devices, per_device(): x = lax.all_gather(block, AXES, axis=0, tiled=True)  58.4 us
    dot_general x2, matrix products, expert_part(): produced = jnp.dot(hidden, w_down, preferred_element_type=jnp.float32)  25.1 us
    all_gather x1, blocking collectives, per_device(): factors = lax.all_gather(spread, AXES, axis=0, tiled=False)  23.5 us
    dot_general x2, matrix products, expert_part(): up_act = jnp.dot(x, w_up, preferred_element_type=jnp.float32)  16.4 us
  transfers between devices with their start and end apart: 4, of which 4 were waited for; matrix products, arithmetic and copies ran while one was open for 16% of the time, Pallas kernels for 0%

profile of v1, /device:TPU:0, one launch (start us, length us, event | category | flops | bytes accessed | tf_op | source)
XLA Modules:
  0.0 273.7 jit_solution(520565956187999122)
XLA Ops:
  6.5 2.0 fusion.20
  8.6 0.0 all-gather.4.cloned.1.call-update
  8.6 0.0 all-gather.6.cloned.1.call-start
  8.6 0.7 all-gather.6.cloned.1.call-update
  9.3 0.0 reduce-scatter.3.cloned.1.call-start
  9.4 0.7 convert_reduce_fusion
  10.1 0.7 convert_divide_fusion
  10.8 0.7 select_reduce_fusion
  11.5 23.5 %all-gather = f32[2048,16]{0,1:T(8,128)S(1)} all-gather(f32[128,16]{0,1:T(8,128)S(1)} %select_reduce_fusion), channel_id=2, replica_groups=mesh['groups'=2,'expert'=8,'dp'=2] {'expert','dp'}, dimensions={0}, use_global_device_ids=true | all-gather | bytes 139264 | tf_op jit(solution)/shard_map/all_gather | solution.py:25
  35.0 0.1 constant_dynamic-slice_fusion
  35.1 0.1 mul.39
  35.2 28.1 %all-gather.4.cloned.1.call-done = bf16[1024,2048]{1,0:T(8,128)(2,1)} async-done(((bf16[64,2048]{1,0:T(8,128)(2,1)}), bf16[1024,2048]{1,0:T(8,128)(2,1)}) %all-gather.4.cloned.1.call-update) | async-done | bytes 4194320 | tf_op jit(solution)/shard_map/all_gather | solution.py:35
  63.2 8.2 %fusion.4 = f32[1024,768]{1,0:T(8,128)} fusion(bf16[1024,2048]{1,0:T(8,128)(2,1)} %all-gather.4.cloned.1.call-done, bf16[1,2048,768]{2,1,0:T(8,128)(2,1)} %param.10), kind=kOutput, calls=%fused_computation.6 | convolution fusion | flops 3221225472 | bytes 10485760 | tf_op jit(solution)/shard_map/dot_general | solution.py:11
  71.5 12.4 %multiply_convert_fusion.1 = bf16[1024,2048]{1,0:T(8,128)(2,1)} fusion(f32[1024]{0:T(1024)S(1)} %mul.39, bf16[1,768,2048]{2,1,0:T(8,128)(2,1)S(1)} %copy-done, f32[1024,768]{1,0:T(8,128)} %fusion.4, bf16[1024,2048]{1,0:T(8,128)(2,1)} %all-gather.4.cloned.1.call-done, bf16[1,2048,768]{2,1,0:T(8,128)(2,1)} %param.9), kind=kOutput, calls=%fused_computation.1 | convolution fusion | flops 6451363840 | bytes 17829888 | tf_op jit(solution)/shard_map/dot_general | solution.py:13
  83.9 0.0 reduce-scatter.3.cloned.1.call-update
  83.9 0.2 reduce-scatter.5.cloned.1.call-start
  84.1 0.1 mul.44
  84.2 30.3 %all-gather.6.cloned.1.call-done = bf16[1024,2048]{1,0:T(8,128)(2,1)} async-done(((bf16[64,2048]{1,0:T(8,128)(2,1)}), bf16[1024,2048]{1,0:T(8,128)(2,1)}) %all-gather.6.cloned.1.call-update) | async-done | bytes 4194320 | tf_op jit(solution)/shard_map/all_gather | solution.py:35
  114.5 8.2 %fusion.2 = f32[1024,768]{1,0:T(8,128)} fusion(bf16[1024,2048]{1,0:T(8,128)(2,1)} %all-gather.6.cloned.1.call-done, bf16[1,2048,768]{2,1,0:T(8,128)(2,1)} %param.10), kind=kOutput, calls=%fused_computation.4 | convolution fusion | flops 3221225472 | bytes 10485760 | tf_op jit(solution)/shard_map/dot_general | solution.py:11
  122.7 12.7 %multiply_convert_fusion = bf16[1024,2048]{1,0:T(8,128)(2,1)} fusion(f32[1024]{0:T(1024)S(1)} %mul.44, bf16[1,768,2048]{2,1,0:T(8,128)(2,1)S(1)} %copy-done, f32[1024,768]{1,0:T(8,128)} %fusion.2, bf16[1024,2048]{1,0:T(8,128)(2,1)} %all-gather.6.cloned.1.call-done, bf16[1,2048,768]{2,1,0:T(8,128)(2,1)} %param.9), kind=kOutput, calls=%fused_computation | convolution fusion | flops 6451363840 | bytes 17829888 | tf_op jit(solution)/shard_map/dot_general | solution.py:13
  135.4 0.0 reduce-scatter.5.cloned.1.call-update
  135.4 54.1 %reduce-scatter.3.cloned.1.call-done = bf16[64,2048]{1,0:T(8,128)(2,1)} async-done(((bf16[1024,2048]{1,0:T(8,128)(2,1)}), bf16[64,2048]{1,0:T(8,128)(2,1)}) %reduce-scatter.3.cloned.1.call-update) | async-done | bytes 262160 | tf_op jit(solution)/shard_map/reduce_scatter | solution.py:37
  189.5 75.8 %reduce-scatter.5.cloned.1.call-done = bf16[64,2048]{1,0:T(8,128)(2,1)} async-done(((bf16[1024,2048]{1,0:T(8,128)(2,1)}), bf16[64,2048]{1,0:T(8,128)(2,1)}) %reduce-scatter.5.cloned.1.call-update) | async-done | bytes 262160 | tf_op jit(solution)/shard_map/reduce_scatter | solution.py:37
  265.3 1.9 pad_maximum_fusion
  (4 shorter events, 0.0 us)
Async XLA Ops:
  6.5 64.9 %copy-start = (bf16[1,768,2048]{2,1,0:T(8,128)(2,1)S(1)}, bf16[1,768,2048]{2,1,0:T(8,128)(2,1)}, u32[]{:S(2)}) copy-start(bf16[1,768,2048]{2,1,0:T(8,128)(2,1)} %param.11) | copy-start | bytes 9437188
  6.5 56.7 %all-gather.4.cloned.1.call-start = ((), (), s32[]{:S(2)}) async-start(), calls=%async_computation.2 | async-start | bytes 4456448 | tf_op jit(solution)/shard_map/all_gather | solution.py:35
  8.6 105.9 %all-gather.6.cloned.1.call-start = ((), (), s32[]{:S(2)}) async-start(), calls=%async_computation.4 | async-start | bytes 4456448 | tf_op jit(solution)/shard_map/all_gather | solution.py:35
  9.3 180.2 %reduce-scatter.3.cloned.1.call-start = ((), (), s32[]{:S(2)}) async-start(), calls=%async_computation.3 | async-start | bytes 4456448 | tf_op jit(solution)/shard_map/reduce_scatter | solution.py:37
  83.9 181.4 %reduce-scatter.5.cloned.1.call-start = ((), (), s32[]{:S(2)}) async-start(), calls=%async_computation.5 | async-start | bytes 4456448 | tf_op jit(solution)/shard_map/reduce_scatter | solution.py:37
Sparse Core Ops, SparseCore 0:
  9.5 53.6 all-gather.3
  65.4 49.0 all-gather.5
  118.3 71.1 reduce-scatter.2
  193.7 71.5 reduce-scatter.4

commit v2 on v1

--- a/solution.py
+++ b/solution.py
@@ -1,6 +1,9 @@
+import functools
 import jax
 import jax.numpy as jnp
 from jax import lax
+from jax.experimental import pallas as pl
+from jax.experimental.pallas import tpu as pltpu
 from jax.sharding import PartitionSpec as P
 
 AXES = ("expert", "dp")
@@ -14,7 +17,7 @@
     return (produced * factor).astype(jnp.bfloat16)
 
 
-def per_device(tokens, routes, gate_levels, w_gate, w_up, w_down):
+def by_collectives(tokens, routes, gate_levels, w_gate, w_up, w_down):
     rows, width = tokens.shape
     devices = lax.axis_size("expert") * lax.axis_size("dp")
     me = lax.axis_index("expert") * lax.axis_size("dp") + lax.axis_index("dp")
@@ -38,6 +41,259 @@
     return jnp.concatenate(results, axis=0)
 
 
+LANES = 128
+VMEM_ROOM = 56 * 1024 * 1024
+
+
+def kernel(
+    n, block_ref, gate_hbm, up_hbm, down_hbm, out_ref,
+    x, w_gate, w_up, w_down, hid, own, sent, sib, run,
+    load_sem, ring_send, ring_recv, pair_send, pair_recv,
+    back_send, back_recv, run_send, run_recv,
+):
+    half_ring = n // 2
+    rows, width = out_ref.shape
+    piece = rows // 2
+    expert = lax.axis_index("expert")
+    core = lax.axis_index("dp")
+    odd, rank = expert % 2, expert // 2
+    place = rank + odd * (n - 1 - 2 * rank)
+
+    def chip_at(p):
+        return 2 * p + (p // half_ring) * (2 * n - 1 - 4 * p)
+
+    right = {"expert": chip_at((place + 1) % n), "dp": core}
+    left = {"expert": chip_at((place + n - 1) % n), "dp": core}
+    other = {"expert": expert, "dp": 1 - core}
+    ways = (right, left)
+    number = expert * 2 + core
+
+    loads = [
+        pltpu.make_async_copy(src, dst, load_sem.at[i])
+        for i, (src, dst) in enumerate(
+            [
+                (block_ref, x.at[0, pl.ds(0, rows)]),
+                (gate_hbm.at[0], w_gate),
+                (up_hbm.at[0], w_up),
+                (down_hbm.at[0], w_down),
+            ]
+        )
+    ]
+    for load in loads:
+        load.start()
+
+    barrier = pltpu.get_barrier_semaphore()
+    for device in (right, left, other):
+        pl.semaphore_signal(barrier, inc=1, device_id=device, device_id_type=pl.DeviceIdType.MESH)
+    pl.semaphore_wait(barrier, 3)
+
+    def slot_of(way, step):
+        return step if way == 0 else (n - step) % n
+
+    def remote(src, dst, send, recv, device):
+        return pltpu.make_async_remote_copy(
+            src_ref=src, dst_ref=dst, send_sem=send, recv_sem=recv,
+            device_id=device, device_id_type=pl.DeviceIdType.MESH,
+        )
+
+    def ring_copy(way, step, part):
+        rows_of = pl.ds(part * piece, piece)
+        return remote(
+            x.at[slot_of(way, step), rows_of], x.at[slot_of(way, step + 1), rows_of],
+            ring_send.at[way, step, part], ring_recv.at[way, step, part], ways[way],
+        )
+
+    def pair_copy(slot, part):
+        return remote(
+            x.at[slot, pl.ds(part * piece, piece)], x.at[slot, pl.ds(rows + part * piece, piece)],
+            pair_send.at[slot, part], pair_recv.at[slot, part], other,
+        )
+
+    def back_copy(slot):
+        return remote(sent.at[slot], sib.at[slot], back_send.at[slot], back_recv.at[slot], other)
+
+    def run_copy(way, hop, part):
+        rows_of = pl.ds(part * piece, piece)
+        return remote(
+            run.at[way, hop, rows_of], run.at[way, hop + 1, rows_of],
+            run_send.at[way, hop, part], run_recv.at[way, hop, part], ways[way],
+        )
+
+    def travels(way, step, part):
+        return step < half_ring - 1 or part == way
+
+    def compute(slot):
+        level = jnp.sum(
+            jnp.where(
+                lax.broadcasted_iota(jnp.int32, (2 * rows, LANES), 1) == number,
+                x[slot, :, width:].astype(jnp.float32), 0.0,
+            ),
+            axis=1, keepdims=True,
+        )
+
+        def hidden_part(i, carry):
+            cols = pl.ds(pl.multiple_of(i * 256, 256), 256)
+            tokens = x[slot, :, :width]
+            g = jnp.dot(tokens, w_gate[:, cols], preferred_element_type=jnp.float32)
+            u = jnp.dot(tokens, w_up[:, cols], preferred_element_type=jnp.float32)
+            hid[:, cols] = (g / (1.0 + jnp.exp(-g)) * u).astype(jnp.bfloat16)
+            return carry
+
+        lax.fori_loop(0, w_gate.shape[1] // 256, hidden_part, 0)
+
+        def output_part(i, carry):
+            cols = pl.ds(pl.multiple_of(i * 256, 256), 256)
+            y = jnp.dot(hid[...], w_down[:, cols], preferred_element_type=jnp.float32) * level
+            own[slot, :, cols] = y[:rows]
+            sent[slot, :, cols] = y[rows:].astype(jnp.bfloat16)
+            return carry
+
+        lax.fori_loop(0, width // 256, output_part, 0)
+
+    def slots_at(step):
+        return [step] if step in (0, half_ring) else [step, n - step]
+
+    def compute_step(step):
+        for slot in slots_at(step):
+            for part in range(2):
+                pair_copy(slot, part).wait_recv()
+        first, count = step, len(slots_at(step))
+
+        def body(i, carry):
+            compute(first + i * (n - 2 * step))
+            return carry
+
+        lax.fori_loop(0, count, body, 0)
+        for slot in slots_at(step):
+            back_copy(slot).start()
+
+    loads[0].wait()
+    for part in range(2):
+        for way in range(2):
+            ring_copy(way, 0, part if way == 0 else 1 - part).start()
+    for part in range(2):
+        pair_copy(0, part).start()
+    for load in loads[1:]:
+        load.wait()
+    for step in range(1, half_ring + 1):
+        compute_step(step - 1)
+        for order in range(2):
+            for way in range(2):
+                part = order if way == 0 else 1 - order
+                if not travels(way, step - 1, part):
+                    continue
+                ring_copy(way, step - 1, part).wait_recv()
+                if step < half_ring and travels(way, step, part):
+                    ring_copy(way, step, part).start()
+                pair_copy(slot_of(way, step), part).start()
+    compute_step(half_ring)
+
+    def here(slot, part):
+        rows_of = pl.ds(part * piece, piece)
+        return own[slot, rows_of] + sib[slot, rows_of].astype(jnp.float32)
+
+    def pass_on(way, hop, part, arrives):
+        slot = (n - (half_ring - hop)) % n if way == 0 else half_ring - hop
+        rows_of = pl.ds(part * piece, piece)
+        total = here(slot, part)
+        if arrives:
+            run_copy(way, hop - 1, part).wait_recv()
+            total = total + run[way, hop, rows_of].astype(jnp.float32)
+        run[way, hop, rows_of] = total.astype(jnp.bfloat16)
+        run_copy(way, hop, part).start()
+
+    for step in range(1, half_ring):
+        if step == half_ring - 1:
+            for slot in slots_at(step):
+                back_copy(slot).wait_recv()
+    back_copy(half_ring).wait_recv()
+    for way in range(2):
+        pass_on(way, 0, way, False)
+    for hop in range(1, half_ring):
+        if hop > 1:
+            for slot in slots_at(half_ring - hop):
+                back_copy(slot).wait_recv()
+        for order in range(2):
+            for way in range(2):
+                part = 1 - way if order == 0 else way
+                pass_on(way, hop, part, hop > 1 or part == way)
+    back_copy(0).wait_recv()
+    for order in range(2):
+        for way in range(2):
+            part = 1 - way if order == 0 else way
+            run_copy(way, half_ring - 1, part).wait_recv()
+    for part in range(2):
+        rows_of = pl.ds(part * piece, piece)
+        total = here(0, part)
+        for way in range(2):
+            total = total + run[way, half_ring, rows_of].astype(jnp.float32)
+        out_ref[rows_of] = total
+
+    for way in range(2):
+        for step in range(half_ring):
+            for part in range(2):
+                if travels(way, step, part):
+                    ring_copy(way, step, part).wait_send()
+        for hop in range(half_ring):
+            for part in range(2):
+                if hop > 0 or part == way:
+                    run_copy(way, hop, part).wait_send()
+    for slot in range(n):
+        for part in range(2):
+            pair_copy(slot, part).wait_send()
+        back_copy(slot).wait_send()
+
+
+def scratch_of(n, rows, width, hidden):
+    half_ring = n // 2
+    arrays = [
+        ((n, 2 * rows, width + LANES), jnp.bfloat16),
+        ((width, hidden), jnp.bfloat16),
+        ((width, hidden), jnp.bfloat16),
+        ((hidden, width), jnp.bfloat16),
+        ((2 * rows, hidden), jnp.bfloat16),
+        ((n, rows, width), jnp.float32),
+        ((n, rows, width), jnp.bfloat16),
+        ((n, rows, width), jnp.bfloat16),
+        ((2, half_ring + 1, rows, width), jnp.bfloat16),
+    ]
+    total = sum(functools.reduce(lambda a, b: a * b, s) * jnp.dtype(t).itemsize for s, t in arrays)
+    sems = [(4,), (2, half_ring, 2), (2, half_ring, 2), (n, 2), (n, 2), (n,), (n,),
+            (2, half_ring, 2), (2, half_ring, 2)]
+    shapes = [pltpu.VMEM(s, t) for s, t in arrays] + [pltpu.SemaphoreType.DMA(s) for s in sems]
+    return shapes, total
+
+
+def per_device(tokens, routes, gate_levels, w_gate, w_up, w_down):
+    rows, width = tokens.shape
+    hidden = w_gate.shape[2]
+    n, cores = lax.axis_size("expert"), lax.axis_size("dp")
+    shapes, total = scratch_of(n, rows, width, hidden)
+    if total > VMEM_ROOM * 9 // 10 or n < 4 or n % 2 or cores != 2 or n * cores > LANES:
+        return by_collectives(tokens, routes, gate_levels, w_gate, w_up, w_down)
+    named = routes[:, :, None] == jnp.arange(LANES, dtype=jnp.int32)[None, None, :]
+    levels = jnp.sum(jnp.where(named, gate_levels[:, :, None], 0), axis=1)
+    block = jnp.concatenate([tokens, levels.astype(jnp.bfloat16)], axis=1)
+    any_space = pl.BlockSpec(memory_space=pl.ANY)
+    mixed = pl.pallas_call(
+        functools.partial(kernel, n),
+        out_shape=jax.ShapeDtypeStruct((rows, width), jnp.float32),
+        in_specs=[any_space] * 4,
+        out_specs=pl.BlockSpec(memory_space=pltpu.VMEM),
+        scratch_shapes=shapes,
+        compiler_params=pltpu.CompilerParams(
+            collective_id=0, has_side_effects=True, vmem_limit_bytes=VMEM_ROOM
+        ),
+        cost_estimate=pl.CostEstimate(
+            flops=12 * n * rows * width * hidden,
+            bytes_accessed=6 * width * hidden,
+            transcendentals=2 * n * rows * hidden,
+        ),
+    )(block, w_gate, w_up, w_down)
+    shares = jnp.sum(gate_levels, axis=1, keepdims=True).astype(jnp.float32)
+    return (mixed / shares).astype(jnp.bfloat16)
+
+
 def solution(mesh):
     token_spec = P(("groups", "expert", "dp"), None)
     weight_spec = P(("expert", "dp"), None, None)

time: 274 us -> 113 us (0.41)
  waiting for transfers between devices: 189 us -> 0 us
  Pallas kernels: 0 us -> 107 us
  matrix products: 41.5 us -> 0 us
  blocking collectives: 23.5 us -> 0 us
  between operations: 13.1 us -> 0.04 us
    reduce_scatter x2 -> x0, waiting for transfers between devices: 130 us -> none  [per_device(): results.append(lax.psum_scatter(y, AXES, scatter_dimension=0, tiled=True))]
    pallas_call x0 -> x1, Pallas kernels: none -> 107 us  [per_device(): pl.pallas_call(functools.partial(kernel, n), out_shape=jax.ShapeDtypeStru...]
    all_gather x2 -> x0, waiting for transfers between devices: 58.4 us -> none  [per_device(): x = lax.all_gather(block, AXES, axis=0, tiled=True)]
    dot_general x4 -> x0, matrix products: 41.5 us -> none  [the longest x2 25.1 us: expert_part(): produced = jnp.dot(hidden, w_down, preferred_element_type=jnp.float32)]
    all_gather x1 -> x0, blocking collectives: 23.5 us -> none  [per_device(): factors = lax.all_gather(spread, AXES, axis=0, tiled=False)]
  transfers between devices with their start and end apart: 4 -> 0, of which waited for: 4 -> 0; matrix products, arithmetic and copies ran while one was open for 16% -> 0% of each run, Pallas kernels for 0% -> 0%
where the time goes in v2:
time: 113 us
  Pallas kernels  107 us (95%)
  other arithmetic  4.45 us (4%)
  local copies, waits for them, and re-layouts  1.58 us (1%)
    pallas_call x1, Pallas kernels, per_device(): pl.pallas_call(functools.partial(kernel, n), out_shape=jax.ShapeDtypeStru...  107 us

profile of v2, /device:TPU:0, one launch (start us, length us, event | category | flops | bytes accessed | tf_op | source)
XLA Modules:
  0.0 113.0 jit_solution(10466240420446790621)
XLA Ops:
  0.0 0.8 copy.10
  0.8 0.8 copy.9
  1.6 0.3 select_reduce_fusion
  1.9 1.9 %pad_maximum_fusion.block_ref = bf16[128,2176]{1,0:T(8,128)(2,1)} fusion(bf16[128,128]{1,0:T(8,128)(2,1)S(1)} %convert_element_type.14, bf16[128,2048]{1,0:T(8,128)(2,1)} %param.6), kind=kLoop, calls=%fused_computation.1 | loop fusion | flops 1114112 | bytes 1114112 | tf_op jit(solution)/shard_map/concatenate | solution.py:276
  3.8 0.0 copy-start
  3.8 106.9 %shard_map.64 = f32[128,2048]{1,0:T(8,128)} custom-call(bf16[128,2176]{1,0:T(8,128)(2,1)} %pad_maximum_fusion.block_ref, bf16[1,2048,768]{2,1,0:T(8,128)(2,1)} %gate_hbm.1, bf16[1,2048,768]{2,1,0:T(8,128)(2,1)} %up_hbm.1, bf16[1,768,2048]{2,1,0:T(8,128)(2,1)} %down_hbm.1), custom_call_target="tpu_custom_call" | custom-call | flops 19327352832 | bytes 9437184 | tf_op jit(solution)/shard_map/pallas_call | solution.py:278
  110.7 0.0 copy-done
  110.8 2.2 %divide_convert_fusion = bf16[128,2048]{1,0:T(8,128)(2,1)} fusion(f32[128,2048]{1,0:T(8,128)} %shard_map.64, f32[128]{0:T(128)S(1)} %convert_element_type.15), kind=kLoop, calls=%fused_computation | loop fusion | flops 524288 | bytes 1573376 | tf_op jit(solution)/shard_map/convert_element_type | solution.py:294
  (3 shorter events, 0.0 us)
Async XLA Ops:
  3.8 106.9 %copy-start = (s32[128,8]{0,1:T(8,128)S(1)}, s32[128,8]{0,1:T(8,128)}, u32[]{:S(2)}) copy-start(s32[128,8]{0,1:T(8,128)} %param.8) | copy-start | bytes 12292

commit v3 on v2

--- a/solution.py
+++ b/solution.py
@@ -46,7 +46,7 @@
 
 
 def kernel(
-    n, block_ref, gate_hbm, up_hbm, down_hbm, out_ref,
+    n, token_hbm, level_hbm, gate_hbm, up_hbm, down_hbm, out_ref,
     x, w_gate, w_up, w_down, hid, own, sent, sib, run,
     load_sem, ring_send, ring_recv, pair_send, pair_recv,
     back_send, back_recv, run_send, run_recv,
@@ -72,7 +72,8 @@
         pltpu.make_async_copy(src, dst, load_sem.at[i])
         for i, (src, dst) in enumerate(
             [
-                (block_ref, x.at[0, pl.ds(0, rows)]),
+                (token_hbm, x.at[0, pl.ds(0, rows), pl.ds(0, width)]),
+                (level_hbm, x.at[0, pl.ds(0, rows), pl.ds(width, LANES)]),
                 (gate_hbm.at[0], w_gate),
                 (up_hbm.at[0], w_up),
                 (down_hbm.at[0], w_down),
@@ -139,7 +140,7 @@
             hid[:, cols] = (g / (1.0 + jnp.exp(-g)) * u).astype(jnp.bfloat16)
             return carry
 
-        lax.fori_loop(0, w_gate.shape[1] // 256, hidden_part, 0)
+        lax.fori_loop(0, w_gate.shape[1] // 256, hidden_part, 0, unroll=True)
 
         def output_part(i, carry):
             cols = pl.ds(pl.multiple_of(i * 256, 256), 256)
@@ -148,7 +149,7 @@
             sent[slot, :, cols] = y[rows:].astype(jnp.bfloat16)
             return carry
 
-        lax.fori_loop(0, width // 256, output_part, 0)
+        lax.fori_loop(0, width // 256, output_part, 0, unroll=True)
 
     def slots_at(step):
         return [step] if step in (0, half_ring) else [step, n - step]
@@ -168,12 +169,13 @@
             back_copy(slot).start()
 
     loads[0].wait()
+    loads[1].wait()
     for part in range(2):
         for way in range(2):
             ring_copy(way, 0, part if way == 0 else 1 - part).start()
     for part in range(2):
         pair_copy(0, part).start()
-    for load in loads[1:]:
+    for load in loads[2:]:
         load.wait()
     for step in range(1, half_ring + 1):
         compute_step(step - 1)
@@ -186,8 +188,6 @@
                 if step < half_ring and travels(way, step, part):
                     ring_copy(way, step, part).start()
                 pair_copy(slot_of(way, step), part).start()
-    compute_step(half_ring)
-
     def here(slot, part):
         rows_of = pl.ds(part * piece, piece)
         return own[slot, rows_of] + sib[slot, rows_of].astype(jnp.float32)
@@ -202,21 +202,22 @@
         run[way, hop, rows_of] = total.astype(jnp.bfloat16)
         run_copy(way, hop, part).start()
 
-    for step in range(1, half_ring):
-        if step == half_ring - 1:
-            for slot in slots_at(step):
-                back_copy(slot).wait_recv()
+    for slot in slots_at(half_ring - 1):
+        back_copy(slot).wait_recv()
+    for way in range(2):
+        pass_on(way, 1, 1 - way, False)
+    compute_step(half_ring)
     back_copy(half_ring).wait_recv()
     for way in range(2):
         pass_on(way, 0, way, False)
-    for hop in range(1, half_ring):
-        if hop > 1:
-            for slot in slots_at(half_ring - hop):
-                back_copy(slot).wait_recv()
+    for way in range(2):
+        pass_on(way, 1, way, True)
+    for hop in range(2, half_ring):
+        for slot in slots_at(half_ring - hop):
+            back_copy(slot).wait_recv()
         for order in range(2):
             for way in range(2):
-                part = 1 - way if order == 0 else way
-                pass_on(way, hop, part, hop > 1 or part == way)
+                pass_on(way, hop, 1 - way if order == 0 else way, True)
     back_copy(0).wait_recv()
     for order in range(2):
         for way in range(2):
@@ -227,7 +228,9 @@
         total = here(0, part)
         for way in range(2):
             total = total + run[way, half_ring, rows_of].astype(jnp.float32)
-        out_ref[rows_of] = total
+        levels = x[0, rows_of, width:].astype(jnp.float32)
+        share = 1.0 / jnp.sum(levels, axis=1, keepdims=True)
+        out_ref[rows_of] = (total * share).astype(jnp.bfloat16)
 
     for way in range(2):
         for step in range(half_ring):
@@ -258,7 +261,7 @@
         ((2, half_ring + 1, rows, width), jnp.bfloat16),
     ]
     total = sum(functools.reduce(lambda a, b: a * b, s) * jnp.dtype(t).itemsize for s, t in arrays)
-    sems = [(4,), (2, half_ring, 2), (2, half_ring, 2), (n, 2), (n, 2), (n,), (n,),
+    sems = [(5,), (2, half_ring, 2), (2, half_ring, 2), (n, 2), (n, 2), (n,), (n,),
             (2, half_ring, 2), (2, half_ring, 2)]
     shapes = [pltpu.VMEM(s, t) for s, t in arrays] + [pltpu.SemaphoreType.DMA(s) for s in sems]
     return shapes, total
@@ -273,12 +276,11 @@
         return by_collectives(tokens, routes, gate_levels, w_gate, w_up, w_down)
     named = routes[:, :, None] == jnp.arange(LANES, dtype=jnp.int32)[None, None, :]
     levels = jnp.sum(jnp.where(named, gate_levels[:, :, None], 0), axis=1)
-    block = jnp.concatenate([tokens, levels.astype(jnp.bfloat16)], axis=1)
     any_space = pl.BlockSpec(memory_space=pl.ANY)
-    mixed = pl.pallas_call(
+    return pl.pallas_call(
         functools.partial(kernel, n),
-        out_shape=jax.ShapeDtypeStruct((rows, width), jnp.float32),
-        in_specs=[any_space] * 4,
+        out_shape=jax.ShapeDtypeStruct((rows, width), jnp.bfloat16),
+        in_specs=[any_space] * 5,
         out_specs=pl.BlockSpec(memory_space=pltpu.VMEM),
         scratch_shapes=shapes,
         compiler_params=pltpu.CompilerParams(
@@ -289,9 +291,7 @@
             bytes_accessed=6 * width * hidden,
             transcendentals=2 * n * rows * hidden,
         ),
-    )(block, w_gate, w_up, w_down)
-    shares = jnp.sum(gate_levels, axis=1, keepdims=True).astype(jnp.float32)
-    return (mixed / shares).astype(jnp.bfloat16)
+    )(tokens, levels.astype(jnp.bfloat16), w_gate, w_up, w_down)
 
 
 def solution(mesh):

time: 113 us -> 101 us (0.89)
  Pallas kernels: 107 us -> 96.3 us
  other arithmetic: 4.45 us -> 0.96 us
  local copies, waits for them, and re-layouts: 1.58 us -> 3.45 us
    pallas_call x1, Pallas kernels: 107 us -> 96.3 us  [per_device(): pl.pallas_call(functools.partial(kernel, n), out_shape=jax.ShapeDtypeStru...]
    concatenate x1 -> x0, other arithmetic: 1.9 us -> none  [per_device(): block = jnp.concatenate([tokens, levels.astype(jnp.bfloat16)], axis=1)]
    unnamed x4 -> x3, local copies, waits for them, and re-layouts: 1.58 us -> 3.45 us
    convert_element_type x3 -> x1, other arithmetic: 2.18 us -> 0.62 us  [per_device(): levels.astype(jnp.bfloat16)]
where the time goes in v3:
time: 101 us
  Pallas kernels  96.3 us (95%)
  local copies, waits for them, and re-layouts  3.45 us (3%)
    pallas_call x1, Pallas kernels, per_device(): pl.pallas_call(functools.partial(kernel, n), out_shape=jax.ShapeDtypeStru...  96.3 us
    unnamed x3, local copies, waits for them, and re-layouts  3.45 us

profile of v3, /device:TPU:0, one launch (start us, length us, event | category | flops | bytes accessed | tf_op | source)
XLA Modules:
  0.0 100.8 jit_solution(10394569327414860410)
XLA Ops:
  0.0 0.8 copy.9
  0.8 0.8 copy.10
  1.6 0.3 select_reduce_fusion
  1.9 0.6 convert_element_type.3.level_hbm
  2.5 96.3 %shard_map.64 = bf16[128,2048]{1,0:T(8,128)(2,1)} custom-call(bf16[128,2048]{1,0:T(8,128)(2,1)} %token_hbm.1, bf16[128,128]{1,0:T(8,128)(2,1)} %convert_element_type.3.level_hbm, bf16[1,2048,768]{2,1,0:T(8,128)(2,1)} %gate_hbm.1, bf16[1,2048,768]{2,1,0:T(8,128)(2,1)} %up_hbm.1, bf16[1,768,2048]{2,1,0:T(8,128)(2,1)} %down_hbm.1), custom_call_target="tpu_custom_call" | custom-call | flops 19327352832 | bytes 9437184 | tf_op jit(solution)/shard_map/pallas_call | solution.py:280
  98.9 1.9 %copy.12 = bf16[128,2048]{1,0:T(8,128)(2,1)} copy(bf16[128,2048]{1,0:T(8,128)(2,1)} %shard_map.64) | data formatting | bytes 1048576

commit v4 on v3

--- a/solution.py
+++ b/solution.py
@@ -47,9 +47,10 @@
 
 def kernel(
     n, token_hbm, level_hbm, gate_hbm, up_hbm, down_hbm, out_ref,
-    x, w_gate, w_up, w_down, hid, own, sent, sib, run,
+    x, lev, w_gate, w_up, w_down, hid, own, sent, sib, run,
     load_sem, ring_send, ring_recv, pair_send, pair_recv,
     back_send, back_recv, run_send, run_recv,
+    lev_send, lev_recv, lev_pair_send, lev_pair_recv,
 ):
     half_ring = n // 2
     rows, width = out_ref.shape
@@ -72,8 +73,8 @@
         pltpu.make_async_copy(src, dst, load_sem.at[i])
         for i, (src, dst) in enumerate(
             [
-                (token_hbm, x.at[0, pl.ds(0, rows), pl.ds(0, width)]),
-                (level_hbm, x.at[0, pl.ds(0, rows), pl.ds(width, LANES)]),
+                (token_hbm, x.at[0, pl.ds(0, rows)]),
+                (level_hbm, lev.at[0, 0]),
                 (gate_hbm.at[0], w_gate),
                 (up_hbm.at[0], w_up),
                 (down_hbm.at[0], w_down),
@@ -104,6 +105,30 @@
             ring_send.at[way, step, part], ring_recv.at[way, step, part], ways[way],
         )
 
+    def level_copy(way, step):
+        return remote(
+            lev.at[slot_of(way, step), 0], lev.at[slot_of(way, step + 1), 0],
+            lev_send.at[way, step], lev_recv.at[way, step], ways[way],
+        )
+
+    def level_travels(way, step):
+        return step < half_ring - way
+
+    def level_pair_copy(slot):
+        return remote(
+            lev.at[slot, 0], lev.at[slot, 1], lev_pair_send.at[slot], lev_pair_recv.at[slot], other
+        )
+
+    def upright(line):
+        across = lax.broadcasted_iota(jnp.int32, (rows, rows), 1)
+        down = lax.broadcasted_iota(jnp.int32, (rows, rows), 0)
+        return jnp.sum(jnp.where(across == down, line, 0.0), axis=1, keepdims=True)
+
+    def level_of(slot, side):
+        table = lev[slot, side].astype(jnp.float32)
+        chosen = lax.broadcasted_iota(jnp.int32, table.shape, 0) == number
+        return upright(jnp.sum(jnp.where(chosen, table, 0.0), axis=0, keepdims=True))
+
     def pair_copy(slot, part):
         return remote(
             x.at[slot, pl.ds(part * piece, piece)], x.at[slot, pl.ds(rows + part * piece, piece)],
@@ -124,17 +149,11 @@
         return step < half_ring - 1 or part == way
 
     def compute(slot):
-        level = jnp.sum(
-            jnp.where(
-                lax.broadcasted_iota(jnp.int32, (2 * rows, LANES), 1) == number,
-                x[slot, :, width:].astype(jnp.float32), 0.0,
-            ),
-            axis=1, keepdims=True,
-        )
+        level = jnp.concatenate([level_of(slot, side) for side in range(2)], axis=0)
 
         def hidden_part(i, carry):
             cols = pl.ds(pl.multiple_of(i * 256, 256), 256)
-            tokens = x[slot, :, :width]
+            tokens = x[slot]
             g = jnp.dot(tokens, w_gate[:, cols], preferred_element_type=jnp.float32)
             u = jnp.dot(tokens, w_up[:, cols], preferred_element_type=jnp.float32)
             hid[:, cols] = (g / (1.0 + jnp.exp(-g)) * u).astype(jnp.bfloat16)
@@ -156,6 +175,7 @@
 
     def compute_step(step):
         for slot in slots_at(step):
+            level_pair_copy(slot).wait_recv()
             for part in range(2):
                 pair_copy(slot, part).wait_recv()
         first, count = step, len(slots_at(step))
@@ -170,6 +190,9 @@
 
     loads[0].wait()
     loads[1].wait()
+    for way in range(2):
+        level_copy(way, 0).start()
+    level_pair_copy(0).start()
     for part in range(2):
         for way in range(2):
             ring_copy(way, 0, part if way == 0 else 1 - part).start()
@@ -179,6 +202,12 @@
         load.wait()
     for step in range(1, half_ring + 1):
         compute_step(step - 1)
+        for way in range(2):
+            if level_travels(way, step - 1):
+                level_copy(way, step - 1).wait_recv()
+                if step < half_ring and level_travels(way, step):
+                    level_copy(way, step).start()
+                level_pair_copy(slot_of(way, step)).start()
         for order in range(2):
             for way in range(2):
                 part = order if way == 0 else 1 - order
@@ -218,6 +247,7 @@
         for order in range(2):
             for way in range(2):
                 pass_on(way, hop, 1 - way if order == 0 else way, True)
+    share = 1.0 / upright(jnp.sum(lev[0, 0].astype(jnp.float32), axis=0, keepdims=True))
     back_copy(0).wait_recv()
     for order in range(2):
         for way in range(2):
@@ -228,12 +258,12 @@
         total = here(0, part)
         for way in range(2):
             total = total + run[way, half_ring, rows_of].astype(jnp.float32)
-        levels = x[0, rows_of, width:].astype(jnp.float32)
-        share = 1.0 / jnp.sum(levels, axis=1, keepdims=True)
-        out_ref[rows_of] = (total * share).astype(jnp.bfloat16)
+        out_ref[rows_of] = (total * share[part * piece : (part + 1) * piece]).astype(jnp.bfloat16)
 
     for way in range(2):
         for step in range(half_ring):
+            if level_travels(way, step):
+                level_copy(way, step).wait_send()
             for part in range(2):
                 if travels(way, step, part):
                     ring_copy(way, step, part).wait_send()
@@ -242,15 +272,17 @@
                 if hop > 0 or part == way:
                     run_copy(way, hop, part).wait_send()
     for slot in range(n):
+        level_pair_copy(slot).wait_send()
         for part in range(2):
             pair_copy(slot, part).wait_send()
         back_copy(slot).wait_send()
 
 
-def scratch_of(n, rows, width, hidden):
+def scratch_of(n, experts, rows, width, hidden):
     half_ring = n // 2
     arrays = [
-        ((n, 2 * rows, width + LANES), jnp.bfloat16),
+        ((n, 2 * rows, width), jnp.bfloat16),
+        ((n, 2, experts, rows), jnp.bfloat16),
         ((width, hidden), jnp.bfloat16),
         ((width, hidden), jnp.bfloat16),
         ((hidden, width), jnp.bfloat16),
@@ -262,7 +294,7 @@
     ]
     total = sum(functools.reduce(lambda a, b: a * b, s) * jnp.dtype(t).itemsize for s, t in arrays)
     sems = [(5,), (2, half_ring, 2), (2, half_ring, 2), (n, 2), (n, 2), (n,), (n,),
-            (2, half_ring, 2), (2, half_ring, 2)]
+            (2, half_ring, 2), (2, half_ring, 2), (2, half_ring), (2, half_ring), (n,), (n,)]
     shapes = [pltpu.VMEM(s, t) for s, t in arrays] + [pltpu.SemaphoreType.DMA(s) for s in sems]
     return shapes, total
 
@@ -271,11 +303,13 @@
     rows, width = tokens.shape
     hidden = w_gate.shape[2]
     n, cores = lax.axis_size("expert"), lax.axis_size("dp")
-    shapes, total = scratch_of(n, rows, width, hidden)
-    if total > VMEM_ROOM * 9 // 10 or n < 4 or n % 2 or cores != 2 or n * cores > LANES:
+    experts = -(-n * cores // 16) * 16
+    shapes, total = scratch_of(n, experts, rows, width, hidden)
+    if total > VMEM_ROOM * 9 // 10 or n < 4 or n % 2 or cores != 2 or rows != LANES:
         return by_collectives(tokens, routes, gate_levels, w_gate, w_up, w_down)
-    named = routes[:, :, None] == jnp.arange(LANES, dtype=jnp.int32)[None, None, :]
-    levels = jnp.sum(jnp.where(named, gate_levels[:, :, None], 0), axis=1)
+    numbers = jnp.arange(experts, dtype=jnp.int32)[:, None, None]
+    named = routes.T[None, :, :] == numbers
+    levels = jnp.sum(jnp.where(named, gate_levels.T[None, :, :], 0), axis=1)
     any_space = pl.BlockSpec(memory_space=pl.ANY)
     return pl.pallas_call(
         functools.partial(kernel, n),

time: 101 us -> 98.1 us (0.971)
  Pallas kernels: 96.3 us -> 94.7 us
  local copies, waits for them, and re-layouts: 3.45 us -> 1.88 us
    pallas_call x1, Pallas kernels: 96.3 us -> 94.7 us  [per_device(): pl.pallas_call(functools.partial(kernel, n), out_shape=jax.ShapeDtypeStru...]
    unnamed x3 -> x1, local copies, waits for them, and re-layouts: 3.45 us -> 1.88 us
where the time goes in v4:
time: 98.1 us; the launch traced here: 97.9 us
  Pallas kernels  94.7 us (97%)
  local copies, waits for them, and re-layouts  1.88 us (2%)
  other arithmetic  1.32 us (1%)
    pallas_call x1, Pallas kernels, per_device(): pl.pallas_call(functools.partial(kernel, n), out_shape=jax.ShapeDtypeStru...  94.7 us

profile of v4, /device:TPU:0, one launch (start us, length us, event | category | flops | bytes accessed | tf_op | source)
XLA Modules:
  0.0 97.9 jit_solution(3064727702039746927)
XLA Ops:
  0.0 0.7 select_reduce_fusion
  0.7 0.6 convert_element_type.3.level_hbm
  1.3 94.7 %shard_map.64 = bf16[128,2048]{1,0:T(8,128)(2,1)} custom-call(bf16[128,2048]{1,0:T(8,128)(2,1)} %token_hbm.1, bf16[16,128]{1,0:T(8,128)(2,1)} %convert_element_type.3.level_hbm, bf16[1,2048,768]{2,1,0:T(8,128)(2,1)} %gate_hbm.1, bf16[1,2048,768]{2,1,0:T(8,128)(2,1)} %up_hbm.1, bf16[1,768,2048]{2,1,0:T(8,128)(2,1)} %down_hbm.1), custom_call_target="tpu_custom_call" | custom-call | flops 19327352832 | bytes 9437184 | tf_op jit(solution)/shard_map/pallas_call | solution.py:314
  96.0 1.9 %copy.8 = bf16[128,2048]{1,0:T(8,128)(2,1)} copy(bf16[128,2048]{1,0:T(8,128)(2,1)} %shard_map.64) | data formatting | bytes 1048576
